TPU v7x, 32 devices: a whole 2x2x4 slice. The times are simulated.
32 devices in a mesh: lat: 8 (over z, y), lon: 4 (over x, core).
Axes of the slice: x: 2, y: 2, z: 4, core: 2. Of those that a mesh axis runs over, the one named last changes fastest.
Arguments:
- thermal_anomaly: float32 [32, 128, 512], P(None, 'lat', 'lon'), may hold values from -6 to 6
- moisture_ratio: float32 [32, 128, 512], P(None, 'lat', 'lon'), may hold values from 0.1 to 1
- zonal_cfl_ratio: float32 [32, 128, 512], P(None, 'lat', 'lon'), may hold values from -0.4 to 0.4
- meridional_cfl_ratio: float32 [32, 128, 512], P(None, 'lat', 'lon'), may hold values from -0.4 to 0.4
- lateral_smoothing_ratio: float32 [32, 128, 512], P(None, 'lat', 'lon'), may hold values from 0.1 to 0.2
- upright_smoothing_ratio: float32 [32, 128, 512], P(None, 'lat', 'lon'), may hold values from 0.3 to 3
- phase_choice: int32 [32, 128, 512], P(None, 'lat', 'lon'), may hold values 0 or 1
- physics_enabled_mask: int32 [128, 512], P('lat', 'lon'), may hold values from 0 to 1, as said below
- group_position_map: int32 [128, 512], P('lat', 'lon'), may hold values from 0 to 65535, as said below
Outputs:
- thermal_final: float32 [32, 128, 512], P(None, 'lat', 'lon')
- moisture_final: float32 [32, 128, 512], P(None, 'lat', 'lon')
- group_cloud_water: float32 [32, 2048], P(('lat', 'lon'))
Inputs may be any that keep to these rules, and one draw needn't show every extreme that they name: `group_position_map`: every value appears once. A column's span is its value // 2048, held by the device of that index along lat+lon, at position value % 2048. Of the columns of one device exactly 32 go to each other device and 1056 stay on the device. `physics_enabled_mask`: every span holds exactly 768 active columns.
All inputs are finite; a program needn't handle non-finite values. No bound on the sum of `phase_choice` on one device may be relied on, other than what follows from the above.
Results may differ from a plain program's by a relative error of at most 0.000088.
Values sent between devices are 32-bit elements; how exact they have to be, the bound alone decides.
A program may use at most 64 MiB of HBM per device.

v0:
```python
import functools

import jax
import jax.numpy as jnp
from jax import lax
from jax.experimental import pallas as pl
from jax.experimental.pallas import tpu as pltpu
from jax.sharding import PartitionSpec as P

NDYN = 4
NSUB = 8
GROUPS = 2
UNROLL = 4
MICRO = 4
MESH = pl.DeviceIdType.MESH
LOG2E = 1.4426950408889634
GAIN = 0.25 * LOG2E
NT = (((1,), (1,)), ((), ()))


def split3(x):
    high = x.astype(jnp.bfloat16)
    rest = x - high.astype(jnp.float32)
    mid = rest.astype(jnp.bfloat16)
    low = (rest - mid.astype(jnp.float32)).astype(jnp.bfloat16)
    return jnp.concatenate([high, mid, low], axis=0)


def join3(x):
    n = x.shape[0] // 3
    return x[:n] + x[n : 2 * n] + x[2 * n :]


def kernel(
    nlat,
    nlon,
    t_in,
    q_in,
    u_in,
    v_in,
    m_in,
    e_in,
    b_in,
    act_in,
    map_in,
    t_out,
    q_out,
    g_out,
    T,
    Q,
    C0,
    CE,
    CW,
    CN,
    CS,
    INV,
    RAT,
    col_to_east,
    col_to_west,
    col_from_west,
    col_from_east,
    row_to_north,
    row_to_south,
    row_from_south,
    row_from_north,
    onehot_t,
    onehot_r,
    onehot_lo,
    got_lo,
    pack2d,
    pos_out,
    pos_got,
    val_out,
    val_got,
    halo_send,
    halo_recv,
    pos_send,
    pos_recv,
    val_send,
    val_recv,
):
    levels, rows, cols = t_in.shape
    n = nlat * nlon
    width = rows * cols
    cap = width // (2 * n)
    per = cols // cap
    bundles = n // per
    glev = levels // GROUPS
    lat = lax.axis_index("lat")
    lon = lax.axis_index("lon")
    me = lat * nlon + lon
    east = lax.rem(lon + 1, nlon)
    west = lax.rem(lon + nlon - 1, nlon)
    north = lax.rem(lat + 1, nlat)
    south = lax.rem(lat + nlat - 1, nlat)
    has_north = lat < nlat - 1
    has_south = lat > 0

    def peer(i):
        d = lax.rem(me + 1 + i, n)
        return d, (d // nlon, lax.rem(d, nlon))

    barrier = pltpu.get_barrier_semaphore()

    @pl.loop(0, n - 1)
    def _(i):
        pl.semaphore_signal(barrier, inc=1, device_id=peer(i)[1], device_id_type=MESH)

    lane = lax.broadcasted_iota(jnp.int32, (rows, cols), 1)
    row = lax.broadcasted_iota(jnp.int32, (rows, cols), 0)

    def halo(kind, s, g):
        if kind == 0:
            src, dst, dev = col_to_east.at[s, g], col_from_west.at[s, g], (lat, east)
        elif kind == 1:
            src, dst, dev = col_to_west.at[s, g], col_from_east.at[s, g], (lat, west)
        else:
            a, b, y = (
                (row_to_north, row_from_south, north)
                if kind == 2
                else (row_to_south, row_from_north, south)
            )
            src, dst, dev = a.at[s, g], b.at[s, g], (y, lon)
            if s > 0:
                src, dst = a.at[s, g, pl.ds(0, 2)], b.at[s, g, pl.ds(0, 2)]
        return pltpu.make_async_remote_copy(
            src_ref=src,
            dst_ref=dst,
            send_sem=halo_send.at[kind, s, g],
            recv_sem=halo_recv.at[kind, s, g],
            device_id=dev,
            device_id_type=MESH,
        )

    def start_halos(s, g):
        pl.when(has_north)(lambda: halo(2, s, g).start())
        pl.when(has_south)(lambda: halo(3, s, g).start())
        halo(0, s, g).start()
        halo(1, s, g).start()

    def wait_halos(s, g):
        halo(0, s, g).wait_recv()
        halo(1, s, g).wait_recv()
        pl.when(has_south)(lambda: halo(2, s, g).wait_recv())
        pl.when(has_north)(lambda: halo(3, s, g).wait_recv())

    def end_halos(s, g):
        halo(0, s, g).wait_send()
        halo(1, s, g).wait_send()
        pl.when(has_north)(lambda: halo(2, s, g).wait_send())
        pl.when(has_south)(lambda: halo(3, s, g).wait_send())

    def put(x, which, k, s, g, l, acc):
        to_east, to_west = acc
        here = lane == which * levels + k
        to_east = jnp.where(here, x[:, cols - 1 : cols], to_east)
        to_west = jnp.where(here, x[:, 0:1], to_west)
        row_to_north[s, g, which, pl.ds(l, 1), :] = x[rows - 1 : rows, :]
        row_to_south[s, g, which, pl.ds(l, 1), :] = x[0:1, :]
        return to_east, to_west

    blank = jnp.zeros((rows, cols), jnp.float32)

    for g in range(GROUPS):

        def pack_body(i, acc, g=g):
            for j in range(UNROLL):
                l = i * UNROLL + j
                k = g * glev + l
                for which, ref in enumerate((t_in, q_in, m_in)):
                    acc = put(ref[k], which, k, 0, g, l, acc)
                to_east, to_west = acc
                x = u_in[k]
                here = lane == 3 * levels + k
                acc = (
                    jnp.where(here, x[:, cols - 1 : cols], to_east),
                    jnp.where(here, x[:, 0:1], to_west),
                )
                x = v_in[k]
                row_to_north[0, g, 3, pl.ds(l, 1), :] = x[rows - 1 : rows, :]
                row_to_south[0, g, 3, pl.ds(l, 1), :] = x[0:1, :]
            return acc

        to_east, to_west = lax.fori_loop(0, glev // UNROLL, pack_body, (blank, blank))
        col_to_east[0, g] = to_east
        col_to_west[0, g] = to_west

    @pl.when(jnp.logical_not(has_north))
    def _():
        row_from_north[...] = jnp.zeros_like(row_from_north)

    @pl.when(jnp.logical_not(has_south))
    def _():
        row_from_south[...] = jnp.zeros_like(row_from_south)

    pl.semaphore_wait(barrier, n - 1)
    for g in range(GROUPS):
        start_halos(0, g)

    shift = width.bit_length() - 1
    low_shift = cols.bit_length() - 1
    slot = map_in[...]
    target = lax.shift_right_logical(slot, shift)
    place = slot & (width - 1)
    place_hi = lax.shift_right_logical(place, low_shift)
    place_lo = place & (cols - 1)
    sub_n = lax.broadcasted_iota(jnp.int32, (n, cols), 0)
    sub_c = lax.broadcasted_iota(jnp.int32, (cols, cols), 0)
    lane_c = lax.broadcasted_iota(jnp.int32, (cols, cols), 1)
    before = (sub_c < lane_c).astype(jnp.bfloat16)
    offset = lax.rem(me, per) * cap
    base = jnp.zeros((n, 1), jnp.float32)
    packed_pos = jnp.zeros((2 * n, cols), jnp.float32)
    for r in range(rows):
        hit = (sub_n == target[r : r + 1, :]).astype(jnp.float32)
        onehot_t[r] = hit
        count = jnp.dot(
            hit.astype(jnp.bfloat16), before, preferred_element_type=jnp.float32
        )
        rank = jnp.sum(hit * (count + base), axis=0, keepdims=True).astype(jnp.int32)
        base = base + jnp.sum(hit, axis=1, keepdims=True)
        spread = (sub_c == rank + offset).astype(jnp.bfloat16)
        onehot_r[r] = spread
        onehot_lo[r] = (sub_c == place_lo[r : r + 1, :]).astype(jnp.bfloat16)
        marked = jnp.concatenate(
            [
                hit * place_hi[r : r + 1, :].astype(jnp.float32),
                hit * place_lo[r : r + 1, :].astype(jnp.float32),
            ],
            axis=0,
        ).astype(jnp.bfloat16)
        packed_pos = packed_pos + lax.dot_general(
            marked, spread, NT, preferred_element_type=jnp.float32
        )
    pack2d[...] = packed_pos[:n] * cols + packed_pos[n:]

    def pos_copy(i):
        d, dev = peer(i)
        return d, lambda slot_from: pltpu.make_async_remote_copy(
            src_ref=pos_out.at[d],
            dst_ref=pos_got.at[slot_from],
            send_sem=pos_send.at[d],
            recv_sem=pos_recv.at[slot_from],
            device_id=dev,
            device_id_type=MESH,
        )

    def val_copy(i):
        d, dev = peer(i)
        return d, lambda slot_from: pltpu.make_async_remote_copy(
            src_ref=val_out.at[d],
            dst_ref=val_got.at[slot_from],
            send_sem=val_send.at[d],
            recv_sem=val_recv.at[slot_from],
            device_id=dev,
            device_id_type=MESH,
        )

    @pl.loop(0, n - 1)
    def _(i):
        d, copy = pos_copy(i)
        pos_out[d] = pack2d[pl.ds(d, 1), :]
        copy(me).start()

    pos_got[me] = jnp.zeros((1, cols), jnp.float32)
    val_got[me] = jnp.zeros((1, cols), jnp.float32)

    def pivot_body(i, carry):
        below, ratio = carry
        for j in range(UNROLL):
            k = i * UNROLL + j
            above = jnp.where(k < levels - 1, e_in[k], 0.0)
            inverse = 1.0 / (1.0 + below + above - below * ratio)
            ratio = above * inverse
            INV[k] = inverse
            RAT[k] = ratio
            below = above
        return below, ratio

    lax.fori_loop(0, levels // UNROLL, pivot_body, (blank, blank))

    at_west = lane == 0
    at_east = lane == cols - 1
    at_south = row == 0
    at_north = row == rows - 1
    wall_n = jnp.where(
        jnp.logical_and(at_north, jnp.logical_not(has_north)), 0.0, 1.0
    )
    wall_s = jnp.where(
        jnp.logical_and(at_south, jnp.logical_not(has_south)), 0.0, 1.0
    )

    def from_west(x, packed, lane_from):
        moved = pltpu.roll(packed, lax.rem(cols - lane_from, cols), 1)
        return jnp.where(at_west, moved, pltpu.roll(x, 1, 1))

    def from_east(x, packed, lane_from):
        moved = pltpu.roll(packed, cols - 1 - lane_from, 1)
        return jnp.where(at_east, moved, pltpu.roll(x, cols - 1, 1))

    def from_south(x, edge):
        return jnp.where(at_south, edge, pltpu.roll(x, 1, 0))

    def from_north(x, edge):
        return jnp.where(at_north, edge, pltpu.roll(x, rows - 1, 0))

    def dynamics(s, g):
        wait_halos(s, g)
        packed_w = col_from_west[s, g]
        packed_e = col_from_east[s, g]

        def body(i, acc):
            for j in range(UNROLL):
                l = i * UNROLL + j
                k = g * glev + l

                def edge(ref, which):
                    return ref[s, g, which, pl.ds(l, 1), :]

                if s == 0:
                    u, v, m = u_in[k], v_in[k], m_in[k]
                    u_w = from_west(u, packed_w, 3 * levels + k)
                    u_e = from_east(u, packed_e, 3 * levels + k)
                    m_w = from_west(m, packed_w, 2 * levels + k)
                    m_e = from_east(m, packed_e, 2 * levels + k)
                    v_s = from_south(v, edge(row_from_south, 3))
                    v_n = from_north(v, edge(row_from_north, 3))
                    m_s = from_south(m, edge(row_from_south, 2))
                    m_n = from_north(m, edge(row_from_north, 2))
                    wind_e, mix_e = 0.25 * (u + u_e), 0.5 * (m + m_e)
                    wind_w, mix_w = 0.25 * (u_w + u), 0.5 * (m_w + m)
                    wind_n, mix_n = 0.25 * (v + v_n) * wall_n, 0.5 * (m + m_n) * wall_n
                    wind_s, mix_s = 0.25 * (v_s + v) * wall_s, 0.5 * (m_s + m) * wall_s
                    ce = mix_e - wind_e
                    cw = mix_w + wind_w
                    cn = mix_n - wind_n
                    cs = mix_s + wind_s
                    c0 = (
                        1.0
                        - (wind_e + mix_e)
                        + (wind_w - mix_w)
                        - (wind_n + mix_n)
                        + (wind_s - mix_s)
                    )
                    C0[k], CE[k], CW[k], CN[k], CS[k] = c0, ce, cw, cn, cs
                else:
                    c0, ce, cw, cn, cs = C0[k], CE[k], CW[k], CN[k], CS[k]
                for which, (source, held) in enumerate(((t_in, T), (q_in, Q))):
                    x = source[k] if s == 0 else held[k]
                    new = (
                        c0 * x
                        + ce * from_east(x, packed_e, which * levels + k)
                        + cw * from_west(x, packed_w, which * levels + k)
                    ) + (
                        cn * from_north(x, edge(row_from_north, which))
                        + cs * from_south(x, edge(row_from_south, which))
                    )
                    held[k] = new
                    if s < NDYN - 1:
                        acc = put(new, which, k, s + 1, g, l, acc)
            return acc

        to_east, to_west = lax.fori_loop(0, glev // UNROLL, body, (blank, blank))
        if s < NDYN - 1:
            col_to_east[s + 1, g] = to_east
            col_to_west[s + 1, g] = to_west
            start_halos(s + 1, g)

    active = act_in[...] > 0

    def micro(g, total):
        def body(i, total):
            first = g * glev + i * MICRO
            q0 = Q[pl.ds(first, MICRO)]
            t0 = T[pl.ds(first, MICRO)]
            branch = b_in[pl.ds(first, MICRO)] > 0
            grow = jnp.where(jnp.logical_and(active[None], branch), 0.3, 0.0)
            fade = jnp.where(jnp.logical_and(active[None], jnp.logical_not(branch)), 0.15, 0.0)
            start = GAIN * t0 - 1.0
            q = q0
            condensed = jnp.zeros_like(q0)
            for _ in range(NSUB):
                saturation = jnp.exp2(start + (2.0 * GAIN) * condensed)
                excess = q - saturation
                change = (grow * jnp.maximum(excess, 0.0)) / (1.0 + saturation) + (
                    fade * jnp.minimum(excess, 0.0)
                )
                q = q - change
                condensed = condensed + change
            Q[pl.ds(first, MICRO)] = q
            T[pl.ds(first, MICRO)] = t0 + 2.0 * condensed
            return total + jnp.sum(condensed, axis=0)

        return lax.fori_loop(0, glev // MICRO, body, total)

    for s in range(NDYN - 1):
        for g in range(GROUPS):
            dynamics(s, g)
    total = blank
    for g in range(GROUPS):
        dynamics(NDYN - 1, g)
        total = micro(g, total)
    precip = total * (4.0 / levels)

    packed = jnp.zeros((3 * n, cols), jnp.float32)
    for r in range(rows):
        packed = packed + lax.dot_general(
            split3(onehot_t[r] * precip[r : r + 1, :]),
            onehot_r[r],
            NT,
            preferred_element_type=jnp.float32,
        )
    pack2d[...] = join3(packed)

    @pl.loop(0, n - 1)
    def _(i):
        d, copy = val_copy(i)
        val_out[d] = pack2d[pl.ds(d, 1), :]
        copy(me).start()

    def forward(i, carry):
        below, t, q = carry
        for j in range(UNROLL):
            k = i * UNROLL + j
            inverse = INV[k]
            t = (T[k] - below * t) * inverse
            q = (Q[k] - below * q) * inverse
            T[k] = t
            Q[k] = q
            below = e_in[k]
        return below, t, q

    lax.fori_loop(0, levels // UNROLL, forward, (blank, blank, blank))

    def backward(i, carry):
        t, q = carry
        for j in range(UNROLL):
            k = levels - 1 - (i * UNROLL + j)
            ratio = RAT[k]
            t = T[k] - ratio * t
            q = Q[k] - ratio * q
            t_out[k] = t
            q_out[k] = q
        return t, q

    lax.fori_loop(0, levels // UNROLL, backward, (blank, blank))

    mine = target == me
    collected = jnp.zeros((3 * rows, cols), jnp.float32)
    for r in range(rows):
        keep = jnp.logical_and(mine[r : r + 1, :], row == place_hi[r : r + 1, :])
        collected = collected + lax.dot_general(
            split3(jnp.where(keep, precip[r : r + 1, :], 0.0)),
            onehot_lo[r],
            NT,
            preferred_element_type=jnp.float32,
        )

    @pl.loop(0, n - 1)
    def _(i):
        d, copy = pos_copy(i)
        copy(d).wait_recv()

    where_got = []
    for b in range(bundles):
        place_f = pos_got[b * per]
        for j in range(1, per):
            place_f = place_f + pos_got[b * per + j]
        place_b = place_f.astype(jnp.int32)
        where_got.append(lax.shift_right_logical(place_b, low_shift))
        got_lo[b] = (sub_c == (place_b & (cols - 1))).astype(jnp.bfloat16)

    @pl.loop(0, n - 1)
    def _(i):
        d, copy = val_copy(i)
        copy(d).wait_recv()

    for b in range(bundles):
        value = val_got[b * per]
        for j in range(1, per):
            value = value + val_got[b * per + j]
        collected = collected + lax.dot_general(
            split3(jnp.where(row == where_got[b], value, 0.0)),
            got_lo[b],
            NT,
            preferred_element_type=jnp.float32,
        )
    g_out[...] = join3(collected)

    for s in range(NDYN):
        for g in range(GROUPS):
            end_halos(s, g)

    @pl.loop(0, n - 1)
    def _(i):
        d, copy = pos_copy(i)
        copy(me).wait_send()
        d, copy = val_copy(i)
        copy(me).wait_send()


def on_device(t, q, u, v, m, e, b, act, slots):
    nlat = lax.axis_size("lat")
    nlon = lax.axis_size("lon")
    levels, rows, cols = t.shape
    n = nlat * nlon
    cap = rows * cols // (2 * n)
    bundles = n // (cols // cap)
    glev = levels // GROUPS
    f32 = jnp.float32
    field = pltpu.VMEM((levels, rows, cols), f32)
    column = pltpu.VMEM((NDYN, GROUPS, rows, cols), f32)
    strip = pltpu.VMEM((NDYN, GROUPS, 4, glev, cols), f32)
    packet = pltpu.VMEM((n, 1, cols), f32)
    vmem = pl.BlockSpec(memory_space=pltpu.VMEM)
    t_new, q_new, water = pl.pallas_call(
        functools.partial(kernel, nlat, nlon),
        out_shape=(
            jax.ShapeDtypeStruct(t.shape, f32),
            jax.ShapeDtypeStruct(t.shape, f32),
            jax.ShapeDtypeStruct((rows, cols), f32),
        ),
        in_specs=[vmem] * 9,
        out_specs=(vmem, vmem, vmem),
        scratch_shapes=[field] * 9
        + [column] * 4
        + [strip] * 4
        + [
            pltpu.VMEM((rows, n, cols), f32),
            pltpu.VMEM((rows, cols, cols), jnp.bfloat16),
            pltpu.VMEM((rows, cols, cols), jnp.bfloat16),
            pltpu.VMEM((bundles, cols, cols), jnp.bfloat16),
            pltpu.VMEM((n, cols), f32),
        ]
        + [packet] * 4
        + [pltpu.SemaphoreType.DMA((4, NDYN, GROUPS))] * 2
        + [pltpu.SemaphoreType.DMA((n,))] * 4,
        compiler_params=pltpu.CompilerParams(
            collective_id=0,
            has_side_effects=True,
            vmem_limit_bytes=48 * 1024 * 1024,
        ),
    )(t, q, u, v, m, e, b, act, slots)
    return t_new, q_new, water.reshape(1, rows * cols)


def solution(mesh):
    grid = P(None, "lat", "lon")
    flat = P("lat", "lon")
    return jax.shard_map(
        on_device,
        mesh=mesh,
        in_specs=(grid,) * 7 + (flat,) * 2,
        out_specs=(grid, grid, P(("lat", "lon"), None)),
        check_vma=False,
    )
```

profile of v0, /device:TPU:0, one launch (start us, length us, event | category | flops | bytes accessed | tf_op | source)
XLA Modules:
  0.0 44.0 jit_solution(10695261971738507272)
XLA Ops:
  0.6 0.0 copy-start
  0.6 0.9 %copy-done = f32[32,16,128]{2,1,0:T(8,128)S(1)} copy-done((f32[32,16,128]{2,1,0:T(8,128)S(1)}, f32[32,16,128]{2,1,0:T(8,128)}, u32[]{:S(2)}) %copy-start) | copy-done | bytes 262168
  1.6 0.0 copy-start.1
  1.6 0.9 %copy-done.1 = f32[32,16,128]{2,1,0:T(8,128)S(1)} copy-done((f32[32,16,128]{2,1,0:T(8,128)S(1)}, f32[32,16,128]{2,1,0:T(8,128)}, u32[]{:S(2)}) %copy-start.1) | copy-done | bytes 262168
  2.5 0.0 copy-start.2
  2.5 0.9 %copy-done.2 = f32[32,16,128]{2,1,0:T(8,128)S(1)} copy-done((f32[32,16,128]{2,1,0:T(8,128)S(1)}, f32[32,16,128]{2,1,0:T(8,128)}, u32[]{:S(2)}) %copy-start.2) | copy-done | bytes 262168
  3.5 0.0 copy-start.3
  3.5 0.9 %copy-done.3 = f32[32,16,128]{2,1,0:T(8,128)S(1)} copy-done((f32[32,16,128]{2,1,0:T(8,128)S(1)}, f32[32,16,128]{2,1,0:T(8,128)}, u32[]{:S(2)}) %copy-start.3) | copy-done | bytes 262168
  4.4 0.0 copy-start.4
  4.4 0.9 %copy-done.4 = f32[32,16,128]{2,1,0:T(8,128)S(1)} copy-done((f32[32,16,128]{2,1,0:T(8,128)S(1)}, f32[32,16,128]{2,1,0:T(8,128)}, u32[]{:S(2)}) %copy-start.4) | copy-done | bytes 262168
  5.4 0.0 copy-start.5
  5.4 0.9 %copy-done.5 = f32[32,16,128]{2,1,0:T(8,128)S(1)} copy-done((f32[32,16,128]{2,1,0:T(8,128)S(1)}, f32[32,16,128]{2,1,0:T(8,128)}, u32[]{:S(2)}) %copy-start.5) | copy-done | bytes 262168
  6.3 0.0 copy-start.6
  6.3 0.9 %copy-done.6 = s32[32,16,128]{2,1,0:T(8,128)S(1)} copy-done((s32[32,16,128]{2,1,0:T(8,128)S(1)}, s32[32,16,128]{2,1,0:T(8,128)}, u32[]{:S(2)}) %copy-start.6) | copy-done | bytes 262168
  7.3 0.0 copy-start.7
  7.3 0.7 %copy-done.7 = s32[16,128]{1,0:T(8,128)S(1)} copy-done((s32[16,128]{1,0:T(8,128)S(1)}, s32[16,128]{1,0:T(8,128)}, u32[]{:S(2)}) %copy-start.7) | copy-done | bytes 8216
  8.0 0.0 copy-start.8
  8.0 0.7 %copy-done.8 = s32[16,128]{1,0:T(8,128)S(1)} copy-done((s32[16,128]{1,0:T(8,128)S(1)}, s32[16,128]{1,0:T(8,128)}, u32[]{:S(2)}) %copy-start.8) | copy-done | bytes 8216
  8.7 33.3 %shard_map.112 = (f32[32,16,128]{2,1,0:T(8,128)S(1)}, f32[32,16,128]{2,1,0:T(8,128)S(1)}, f32[16,128]{1,0:T(8,128)S(1)}) custom-call(f32[32,16,128]{2,1,0:T(8,128)S(1)} %copy-done, f32[32,16,128]{2,1,0:T(8,128)S(1)} %copy-done.1, f32[32,16,128]{2,1,0:T(8,128)S(1)} %copy-done.2, f32[32,16,128]{2,1,0:T(8,128)S(1)} %copy-done.3, f32[32,16,128]{2,1,0:T(8,128)S(1)} %copy-done.4, ...), custom_call_target="tpu_custom_call" | custom-call | tf_op jit(solution)/shard_map/pallas_call | solution.py:516
  42.0 0.7 %copy.15 = f32[32,16,128]{2,1,0:T(8,128)} copy(f32[32,16,128]{2,1,0:T(8,128)S(1)} %get-tuple-element.12) | data formatting | bytes 524288
  42.7 0.7 %copy.16 = f32[32,16,128]{2,1,0:T(8,128)} copy(f32[32,16,128]{2,1,0:T(8,128)S(1)} %get-tuple-element.13) | data formatting | bytes 524288
  43.4 0.6 %copy.17 = f32[1,2048]{1,0:T(1,128)} copy(f32[1,2048]{1,0:T(1,128)S(1)} %bitcast.1) | data formatting | bytes 16384
Async XLA Ops:
  0.6 1.0 %copy-start = (f32[32,16,128]{2,1,0:T(8,128)S(1)}, f32[32,16,128]{2,1,0:T(8,128)}, u32[]{:S(2)}) copy-start(f32[32,16,128]{2,1,0:T(8,128)} %t_in.1) | copy-start | bytes 786436
  1.6 0.9 %copy-start.1 = (f32[32,16,128]{2,1,0:T(8,128)S(1)}, f32[32,16,128]{2,1,0:T(8,128)}, u32[]{:S(2)}) copy-start(f32[32,16,128]{2,1,0:T(8,128)} %q_in.1) | copy-start | bytes 786436
  2.5 0.9 %copy-start.2 = (f32[32,16,128]{2,1,0:T(8,128)S(1)}, f32[32,16,128]{2,1,0:T(8,128)}, u32[]{:S(2)}) copy-start(f32[32,16,128]{2,1,0:T(8,128)} %u_in.1) | copy-start | bytes 786436
  3.5 0.9 %copy-start.3 = (f32[32,16,128]{2,1,0:T(8,128)S(1)}, f32[32,16,128]{2,1,0:T(8,128)}, u32[]{:S(2)}) copy-start(f32[32,16,128]{2,1,0:T(8,128)} %v_in.1) | copy-start | bytes 786436
  4.4 0.9 %copy-start.4 = (f32[32,16,128]{2,1,0:T(8,128)S(1)}, f32[32,16,128]{2,1,0:T(8,128)}, u32[]{:S(2)}) copy-start(f32[32,16,128]{2,1,0:T(8,128)} %m_in.1) | copy-start | bytes 786436
  5.4 0.9 %copy-start.5 = (f32[32,16,128]{2,1,0:T(8,128)S(1)}, f32[32,16,128]{2,1,0:T(8,128)}, u32[]{:S(2)}) copy-start(f32[32,16,128]{2,1,0:T(8,128)} %e_in.1) | copy-start | bytes 786436
  6.3 0.9 %copy-start.6 = (s32[32,16,128]{2,1,0:T(8,128)S(1)}, s32[32,16,128]{2,1,0:T(8,128)}, u32[]{:S(2)}) copy-start(s32[32,16,128]{2,1,0:T(8,128)} %b_in.1) | copy-start | bytes 786436
  7.3 0.7 %copy-start.7 = (s32[16,128]{1,0:T(8,128)S(1)}, s32[16,128]{1,0:T(8,128)}, u32[]{:S(2)}) copy-start(s32[16,128]{1,0:T(8,128)} %act_in.1) | copy-start | bytes 24580
  8.0 0.7 %copy-start.8 = (s32[16,128]{1,0:T(8,128)S(1)}, s32[16,128]{1,0:T(8,128)}, u32[]{:S(2)}) copy-start(s32[16,128]{1,0:T(8,128)} %map_in.1) | copy-start | bytes 24580
where the time goes:
time: 44.4 us; the launch traced here: 44 us
  Pallas kernels  33.3 us (75%)
  local copies, waits for them, and re-layouts  10 us (23%)
  between operations  0.66 us (1%)
    pallas_call x1, Pallas kernels, on_device(): pl.pallas_call(functools.partial(kernel, nlat, nlon), out_shape=(jax.Shap...  33.3 us
    unnamed x21, local copies, waits for them, and re-layouts  10 us

commit v1 on v0

v1 whole, which is shorter than its diff:
```python
import functools

import jax
import jax.numpy as jnp
from jax import lax
from jax.experimental import pallas as pl
from jax.experimental.pallas import tpu as pltpu
from jax.sharding import PartitionSpec as P

NDYN = 4
NSUB = 8
GROUPS = 2
UNROLL = 2
MICRO = 4
SOLVE = 4
MESH = pl.DeviceIdType.MESH
LOG2E = 1.4426950408889634
GAIN = 0.25 * LOG2E
NT = (((1,), (1,)), ((), ()))


def split3(x):
    high = x.astype(jnp.bfloat16)
    rest = x - high.astype(jnp.float32)
    mid = rest.astype(jnp.bfloat16)
    low = (rest - mid.astype(jnp.float32)).astype(jnp.bfloat16)
    return jnp.concatenate([high, mid, low], axis=0)


def join3(x):
    n = x.shape[0] // 3
    return x[:n] + x[n : 2 * n] + x[2 * n :]


def kernel(
    nlat,
    nlon,
    levels,
    rows,
    t_hbm,
    q_hbm,
    u_hbm,
    v_hbm,
    m_hbm,
    e_hbm,
    b_hbm,
    act_hbm,
    map_hbm,
    t_out,
    q_out,
    g_out,
    t_in,
    q_in,
    u_in,
    v_in,
    m_in,
    e_in,
    b_in,
    act_in,
    map_in,
    load_sem,
    first,
    later,
    wind,
    C0,
    CE,
    CW,
    CN,
    CS,
    T,
    Q,
    INV,
    RAT,
    col_out,
    col_from_west,
    col_from_east,
    rain,
    onehot_t,
    onehot_r,
    onehot_lo,
    pack2d,
    packet_out,
    packet_got,
    halo_send,
    halo_recv,
    packet_send,
    packet_recv,
):
    cols = t_hbm.shape[1]
    n = nlat * nlon
    width = rows * cols
    cap = width // (2 * n)
    per = cols // cap
    bundles = n // per
    glev = levels // GROUPS
    lat = lax.axis_index("lat")
    lon = lax.axis_index("lon")
    me = lat * nlon + lon
    east = lax.rem(lon + 1, nlon)
    west = lax.rem(lon + nlon - 1, nlon)
    north = lax.rem(lat + 1, nlat)
    south = lax.rem(lat + nlat - 1, nlat)
    has_north = lat < nlat - 1
    has_south = lat > 0

    def peer(i):
        d = lax.rem(me + 1 + i, n)
        return d, (d // nlon, lax.rem(d, nlon))

    loads = {}
    for i, (source, held) in enumerate(
        (
            (t_hbm, t_in),
            (q_hbm, q_in),
            (m_hbm, m_in),
            (u_hbm, u_in),
            (v_hbm, v_in),
            (map_hbm, map_in),
            (e_hbm, e_in),
            (act_hbm, act_in),
            (b_hbm, b_in),
        )
    ):
        loads[i] = pltpu.make_async_copy(source, held, load_sem.at[i])
        loads[i].start()

    barrier = pltpu.get_barrier_semaphore()

    @pl.loop(0, n - 1)
    def _(i):
        pl.semaphore_signal(barrier, inc=1, device_id=peer(i)[1], device_id_type=MESH)

    def state(s, which):
        return first.at[which] if s == 0 else later.at[s - 1, which]

    def halo(kind, s, g):
        part = pl.ds(g * glev, glev)
        if kind == 0:
            src, dst, dev = col_out.at[s, g], col_from_west.at[s, g], (lat, east)
        elif kind == 1:
            src, dst, dev = col_out.at[s, g], col_from_east.at[s, g], (lat, west)
        else:
            ref = first if s == 0 else later.at[s - 1]
            source, target, y = (rows, 0, north) if kind == 2 else (1, rows + 1, south)
            src, dst, dev = ref.at[:, source, part], ref.at[:, target, part], (y, lon)
        return pltpu.make_async_remote_copy(
            src_ref=src,
            dst_ref=dst,
            send_sem=halo_send.at[kind, s, g],
            recv_sem=halo_recv.at[kind, s, g],
            device_id=dev,
            device_id_type=MESH,
        )

    def start_halos(s, g):
        pl.when(has_north)(lambda: halo(2, s, g).start())
        pl.when(has_south)(lambda: halo(3, s, g).start())
        halo(0, s, g).start()
        halo(1, s, g).start()

    def wait_halos(s, g):
        halo(0, s, g).wait_recv()
        halo(1, s, g).wait_recv()
        pl.when(has_south)(lambda: halo(2, s, g).wait_recv())
        pl.when(has_north)(lambda: halo(3, s, g).wait_recv())

    def end_halos(s, g):
        halo(0, s, g).wait_send()
        halo(1, s, g).wait_send()
        pl.when(has_north)(lambda: halo(2, s, g).wait_send())
        pl.when(has_south)(lambda: halo(3, s, g).wait_send())

    lane = lax.broadcasted_iota(jnp.int32, (glev, cols), 1)
    pair = (lane + 1) // 2
    pair = jnp.where(lane == cols - 1, 0, pair)
    at_west = lane == 0
    at_east = lane == cols - 1

    def put(x, p, packed):
        return jnp.where(pair == p, pltpu.roll(x, 2 * p, 1), packed)

    blank = jnp.zeros((glev, cols), jnp.float32)

    @pl.when(jnp.logical_not(has_north))
    def _():
        first[:, rows + 1] = jnp.zeros_like(first[:, rows + 1])
        later[:, :, rows + 1] = jnp.zeros_like(later[:, :, rows + 1])

    @pl.when(jnp.logical_not(has_south))
    def _():
        first[:, 0] = jnp.zeros_like(first[:, 0])
        later[:, :, 0] = jnp.zeros_like(later[:, :, 0])

    for i in range(5):
        loads[i].wait()

    for g in range(GROUPS):

        def arrange(i, packed, g=g):
            for j in range(UNROLL):
                r = i * UNROLL + j
                spots = pl.ds(g * glev * rows + r, glev, rows)
                part = pl.ds(g * glev, glev)
                for which, ref in enumerate((t_in, q_in, m_in)):
                    x = ref[spots, :]
                    first[which, r + 1, part] = x
                    packed = put(x, which * rows + r, packed)
                x = u_in[spots, :]
                wind[r, part] = x
                packed = put(x, 3 * rows + r, packed)
                first[3, r + 1, part] = v_in[spots, :]
            return packed

        col_out[0, g] = lax.fori_loop(0, rows // UNROLL, arrange, blank)

    loads[6].wait()
    plane = jnp.zeros((rows, cols), jnp.float32)

    def level(k):
        return pl.ds(pl.multiple_of(k * rows, rows), rows)

    def pivot_body(i, carry):
        below, ratio = carry
        for j in range(SOLVE):
            k = i * SOLVE + j
            above = jnp.where(k < levels - 1, e_in[level(k), :], 0.0)
            inverse = 1.0 / (1.0 + below + above - below * ratio)
            ratio = above * inverse
            INV[level(k), :] = inverse
            RAT[level(k), :] = ratio
            below = above
        return below, ratio

    def pivots():
        lax.fori_loop(0, levels // SOLVE, pivot_body, (plane, plane))

    loads[5].wait()
    shift = width.bit_length() - 1
    low_shift = cols.bit_length() - 1
    slot = map_in[...]
    target = lax.shift_right_logical(slot, shift)
    place = slot & (width - 1)
    place_hi = lax.shift_right_logical(place, low_shift)
    place_lo = place & (cols - 1)
    sub_n = lax.broadcasted_iota(jnp.int32, (n, cols), 0)
    sub_c = lax.broadcasted_iota(jnp.int32, (cols, cols), 0)
    sub_r = lax.broadcasted_iota(jnp.int32, (rows, cols), 0)
    lane_c = lax.broadcasted_iota(jnp.int32, (cols, cols), 1)
    before = (sub_c < lane_c).astype(jnp.bfloat16)
    offset = lax.rem(me, per) * cap

    def slots(some, carry):
        base, packed_pos = carry
        for r in some:
            hit = (sub_n == target[r : r + 1, :]).astype(jnp.float32)
            onehot_t[r] = hit
            count = jnp.dot(
                hit.astype(jnp.bfloat16), before, preferred_element_type=jnp.float32
            )
            rank = jnp.sum(hit * (count + base), axis=0, keepdims=True).astype(jnp.int32)
            base = base + jnp.sum(hit, axis=1, keepdims=True)
            spread = (sub_c == rank + offset).astype(jnp.bfloat16)
            onehot_r[r] = spread
            onehot_lo[r] = (sub_c == place_lo[r : r + 1, :]).astype(jnp.bfloat16)
            marked = jnp.concatenate(
                [
                    hit * place_hi[r : r + 1, :].astype(jnp.float32),
                    hit * place_lo[r : r + 1, :].astype(jnp.float32),
                ],
                axis=0,
            ).astype(jnp.bfloat16)
            packed_pos = packed_pos + lax.dot_general(
                marked, spread, NT, preferred_element_type=jnp.float32
            )
        return base, packed_pos

    quarter = rows // 4
    sorting = (jnp.zeros((n, 1), jnp.float32), jnp.zeros((2 * n, cols), jnp.float32))
    pivots()
    pl.semaphore_wait(barrier, n - 1)
    for g in range(GROUPS):
        start_halos(0, g)
    sorting = slots(range(quarter), sorting)

    def dynamics(s, g):
        wait_halos(s, g)
        even = lax.rem(lane, 2) == 0
        edges = jnp.where(
            even,
            pltpu.roll(col_from_west[s, g], 1, 1),
            pltpu.roll(col_from_east[s, g], cols - 1, 1),
        )
        part = pl.ds(g * glev, glev)

        def sides(x, p):
            edge = pltpu.roll(edges, lax.rem(cols - 2 * p, cols), 1)
            return (
                jnp.where(at_west, edge, pltpu.roll(x, 1, 1)),
                jnp.where(at_east, edge, pltpu.roll(x, cols - 1, 1)),
            )

        def body(i, packed):
            for j in range(UNROLL):
                r = i * UNROLL + j
                if s == 0:
                    wall_n = jnp.where(
                        jnp.logical_and(r == rows - 1, jnp.logical_not(has_north)), 0.0, 1.0
                    )
                    wall_s = jnp.where(
                        jnp.logical_and(r == 0, jnp.logical_not(has_south)), 0.0, 1.0
                    )
                    m = first[2, r + 1, part]
                    m_s = first[2, r, part]
                    m_n = first[2, r + 2, part]
                    v = first[3, r + 1, part]
                    v_s = first[3, r, part]
                    v_n = first[3, r + 2, part]
                    u = wind[r, part]
                    u_w, u_e = sides(u, 3 * rows + r)
                    m_w, m_e = sides(m, 2 * rows + r)
                    wind_e, mix_e = 0.25 * (u + u_e), 0.5 * (m + m_e)
                    wind_w, mix_w = 0.25 * (u_w + u), 0.5 * (m_w + m)
                    wind_n, mix_n = 0.25 * (v + v_n) * wall_n, 0.5 * (m + m_n) * wall_n
                    wind_s, mix_s = 0.25 * (v_s + v) * wall_s, 0.5 * (m_s + m) * wall_s
                    ce = mix_e - wind_e
                    cw = mix_w + wind_w
                    cn = mix_n - wind_n
                    cs = mix_s + wind_s
                    c0 = (
                        1.0
                        - (wind_e + mix_e)
                        + (wind_w - mix_w)
                        - (wind_n + mix_n)
                        + (wind_s - mix_s)
                    )
                    C0[r, part] = c0
                    CE[r, part] = ce
                    CW[r, part] = cw
                    CN[r, part] = cn
                    CS[r, part] = cs
                else:
                    c0 = C0[r, part]
                    ce = CE[r, part]
                    cw = CW[r, part]
                    cn = CN[r, part]
                    cs = CS[r, part]
                for which in range(2):
                    ref = state(s, which)
                    x = ref[r + 1, part]
                    x_w, x_e = sides(x, which * rows + r)
                    new = (c0 * x + ce * x_e + cw * x_w) + (
                        cn * ref[r + 2, part] + cs * ref[r, part]
                    )
                    if s < NDYN - 1:
                        later[s, which, r + 1, part] = new
                        packed = put(new, which * rows + r, packed)
                    else:
                        (T, Q)[which][pl.ds(pl.multiple_of(r * levels + g * glev, 8), glev), :] = new
            return packed

        packed = lax.fori_loop(0, rows // UNROLL, body, blank)
        if s < NDYN - 1:
            col_out[s + 1, g] = packed
            start_halos(s + 1, g)

    loads[7].wait()
    loads[8].wait()

    def micro(g):
        def body(i, carry):
            for j in range(MICRO // 2):
                r = i * (MICRO // 2) + j
                spots = pl.ds(pl.multiple_of(r * levels + g * glev, 8), glev)
                q0 = Q[spots, :]
                t0 = T[spots, :]
                branch = b_in[pl.ds(g * glev * rows + r, glev, rows), :] > 0
                active = act_in[pl.ds(r, 1), :] > 0
                grow = jnp.where(jnp.logical_and(active, branch), 0.3, 0.0)
                fade = jnp.where(jnp.logical_and(active, jnp.logical_not(branch)), 0.15, 0.0)
                start = GAIN * t0 - 1.0
                q = q0
                condensed = jnp.zeros_like(q0)
                for _ in range(NSUB):
                    saturation = jnp.exp2(start + (2.0 * GAIN) * condensed)
                    excess = q - saturation
                    change = (grow * jnp.maximum(excess, 0.0)) / (1.0 + saturation) + (
                        fade * jnp.minimum(excess, 0.0)
                    )
                    q = q - change
                    condensed = condensed + change
                Q[spots, :] = q
                T[spots, :] = t0 + 2.0 * condensed
                rain[g, pl.ds(r, 1), :] = jnp.sum(condensed, axis=0, keepdims=True)
            return carry

        lax.fori_loop(0, rows // (MICRO // 2), body, 0)

    for s in range(NDYN - 1):
        for g in range(GROUPS):
            dynamics(s, g)
        sorting = slots(range((s + 1) * quarter, (s + 2) * quarter), sorting)
    packed_pos = sorting[1]
    pack2d[:n] = packed_pos[:n] * cols + packed_pos[n:]
    for g in range(GROUPS):
        dynamics(NDYN - 1, g)
        micro(g)
    precip = jnp.sum(rain[...], axis=0) * (4.0 / levels)

    packed = jnp.zeros((3 * n, cols), jnp.float32)
    for r in range(rows):
        packed = packed + lax.dot_general(
            split3(onehot_t[r] * precip[r : r + 1, :]),
            onehot_r[r],
            NT,
            preferred_element_type=jnp.float32,
        )
    pack2d[n:] = join3(packed)

    def packet(i):
        d, dev = peer(i)
        return d, pltpu.make_async_remote_copy(
            src_ref=packet_out.at[d],
            dst_ref=packet_got.at[me],
            send_sem=packet_send.at[d],
            recv_sem=packet_recv.at[me],
            device_id=dev,
            device_id_type=MESH,
        )

    @pl.loop(0, n - 1)
    def _(i):
        d, copy = packet(i)
        packet_out[d, 0:1] = pack2d[pl.ds(d, 1), :]
        packet_out[d, 1:2] = pack2d[pl.ds(n + d, 1), :]
        copy.start()

    packet_got[me] = jnp.zeros(packet_got.shape[1:], jnp.float32)

    def forward(i, carry):
        below, t, q = carry
        for j in range(SOLVE):
            k = i * SOLVE + j
            inverse = INV[level(k), :]
            t = (T[pl.ds(k, rows, levels), :] - below * t) * inverse
            q = (Q[pl.ds(k, rows, levels), :] - below * q) * inverse
            t_in[level(k), :] = t
            q_in[level(k), :] = q
            below = e_in[level(k), :]
        return below, t, q

    lax.fori_loop(0, levels // SOLVE, forward, (plane, plane, plane))

    def backward(i, carry):
        t, q = carry
        for j in range(SOLVE):
            k = levels - 1 - (i * SOLVE + j)
            ratio = RAT[level(k), :]
            t = t_in[level(k), :] - ratio * t
            q = q_in[level(k), :] - ratio * q
            t_out[level(k), :] = t
            q_out[level(k), :] = q
        return t, q

    lax.fori_loop(0, levels // SOLVE, backward, (plane, plane))

    mine = target == me
    collected = jnp.zeros((3 * rows, cols), jnp.float32)
    for r in range(rows):
        keep = jnp.logical_and(mine[r : r + 1, :], sub_r == place_hi[r : r + 1, :])
        collected = collected + lax.dot_general(
            split3(jnp.where(keep, precip[r : r + 1, :], 0.0)),
            onehot_lo[r],
            NT,
            preferred_element_type=jnp.float32,
        )

    @pl.loop(0, n - 1)
    def _(i):
        d = peer(i)[0]
        pltpu.make_async_copy(packet_got.at[d], packet_got.at[d], packet_recv.at[d]).wait()

    for b in range(bundles):
        both = packet_got[b * per]
        for j in range(1, per):
            both = both + packet_got[b * per + j]
        place_b = both[0:1].astype(jnp.int32)
        got_hi = lax.shift_right_logical(place_b, low_shift)
        got_low = (sub_c == (place_b & (cols - 1))).astype(jnp.bfloat16)
        collected = collected + lax.dot_general(
            split3(jnp.where(sub_r == got_hi, both[1:2], 0.0)),
            got_low,
            NT,
            preferred_element_type=jnp.float32,
        )
    g_out[...] = join3(collected)

    for s in range(NDYN):
        for g in range(GROUPS):
            end_halos(s, g)

    @pl.loop(0, n - 1)
    def _(i):
        packet(i)[1].wait_send()


def on_device(t, q, u, v, m, e, b, act, slots):
    nlat = lax.axis_size("lat")
    nlon = lax.axis_size("lon")
    levels, rows, cols = t.shape
    n = nlat * nlon
    glev = levels // GROUPS
    f32 = jnp.float32
    flat = pltpu.VMEM((levels * rows, cols), f32)
    field = pltpu.VMEM((rows, levels, cols), f32)
    column = pltpu.VMEM((NDYN, GROUPS, glev, cols), f32)
    vmem = pl.BlockSpec(memory_space=pltpu.VMEM)
    t_new, q_new, water = pl.pallas_call(
        functools.partial(kernel, nlat, nlon, levels, rows),
        out_shape=(
            jax.ShapeDtypeStruct((levels * rows, cols), f32),
            jax.ShapeDtypeStruct((levels * rows, cols), f32),
            jax.ShapeDtypeStruct((rows, cols), f32),
        ),
        in_specs=[pl.BlockSpec(memory_space=pltpu.HBM)] * 9,
        out_specs=(vmem, vmem, vmem),
        scratch_shapes=[flat] * 6
        + [pltpu.VMEM((levels * rows, cols), jnp.int32)]
        + [pltpu.VMEM((rows, cols), jnp.int32)] * 2
        + [pltpu.SemaphoreType.DMA((9,))]
        + [
            pltpu.VMEM((4, rows + 2, levels, cols), f32),
            pltpu.VMEM((NDYN - 1, 2, rows + 2, levels, cols), f32),
        ]
        + [field] * 6
        + [flat] * 4
        + [column] * 3
        + [
            pltpu.VMEM((GROUPS, rows, cols), f32),
            pltpu.VMEM((rows, n, cols), f32),
            pltpu.VMEM((rows, cols, cols), jnp.bfloat16),
            pltpu.VMEM((rows, cols, cols), jnp.bfloat16),
            pltpu.VMEM((2 * n, cols), f32),
            pltpu.VMEM((n, 2, cols), f32),
            pltpu.VMEM((n, 2, cols), f32),
        ]
        + [pltpu.SemaphoreType.DMA((4, NDYN, GROUPS))] * 2
        + [pltpu.SemaphoreType.DMA((n,))] * 2,
        compiler_params=pltpu.CompilerParams(collective_id=0, has_side_effects=True),
    )(*(x.reshape(levels * rows, cols) for x in (t, q, u, v, m, e, b)), act, slots)
    return t_new.reshape(t.shape), q_new.reshape(t.shape), water.reshape(1, rows * cols)


def solution(mesh):
    grid = P(None, "lat", "lon")
    flat = P("lat", "lon")
    return jax.shard_map(
        on_device,
        mesh=mesh,
        in_specs=(grid,) * 7 + (flat,) * 2,
        out_specs=(grid, grid, P(("lat", "lon"), None)),
        check_vma=False,
    )
```

time: 44.4 us -> 40.9 us (0.921)
  local copies, waits for them, and re-layouts: 10 us -> 3.02 us
  Pallas kernels: 33.3 us -> 37 us
    unnamed x21 -> x7, local copies, waits for them, and re-layouts: 10 us -> 3.02 us
    pallas_call x1, Pallas kernels: 33.3 us -> 37 us  [on_device(): pl.pallas_call(functools.partial(kernel, nlat, nlon, levels, rows), out_s...]
where the time goes in v1:
time: 40.9 us; the launch traced here: 40.7 us
  Pallas kernels  37 us (90%)
  local copies, waits for them, and re-layouts  3.02 us (7%)
  between operations  0.65 us (2%)
    pallas_call x1, Pallas kernels, on_device(): pl.pallas_call(functools.partial(kernel, nlat, nlon, levels, rows), out_s...  37 us
    unnamed x7, local copies, waits for them, and re-layouts  3.02 us

profile of v1, /device:TPU:0, one launch (start us, length us, event | category | flops | bytes accessed | tf_op | source)
XLA Modules:
  0.0 40.7 jit_solution(6680730992049715155)
XLA Ops:
  0.6 37.0 %shard_map.112 = (f32[512,128]{1,0:T(8,128)}, f32[512,128]{1,0:T(8,128)}, f32[16,128]{1,0:T(8,128)}) custom-call(f32[512,128]{1,0:T(8,128)} %bitcast.10, f32[512,128]{1,0:T(8,128)} %bitcast.11, f32[512,128]{1,0:T(8,128)} %bitcast.12, f32[512,128]{1,0:T(8,128)} %bitcast.13, f32[512,128]{1,0:T(8,128)} %bitcast.14, f32[512,128]{1,0:T(8,128)} %bitcast.15, ...), custom_call_target="tpu_custom_call" | custom-call | tf_op jit(solution)/shard_map/pallas_call | solution.py:517
  37.6 0.0 copy-start
  37.6 1.7 %copy.15 = f32[32,16,128]{2,1,0:T(8,128)} copy(f32[32,16,128]{2,1,0:T(8,128)} %bitcast.18) | data formatting | bytes 524288
  39.4 0.0 copy-done
  39.4 0.0 copy-start.1
  39.4 0.7 %copy.16 = f32[32,16,128]{2,1,0:T(8,128)} copy(f32[32,16,128]{2,1,0:T(8,128)S(1)} %bitcast.17) | data formatting | bytes 524288
  40.1 0.0 copy-done.1
  40.1 0.6 %copy.17 = f32[1,2048]{1,0:T(1,128)} copy(f32[1,2048]{1,0:T(1,128)S(1)} %bitcast.19) | data formatting | bytes 16384
Async XLA Ops:
  37.6 1.7 %copy-start = (f32[512,128]{1,0:T(8,128)S(1)}, f32[512,128]{1,0:T(8,128)}, u32[]{:S(2)}) copy-start(f32[512,128]{1,0:T(8,128)} %get-tuple-element.7) | copy-start | bytes 786436
  39.4 0.7 %copy-start.1 = (f32[16,128]{1,0:T(8,128)S(1)}, f32[16,128]{1,0:T(8,128)}, u32[]{:S(2)}) copy-start(f32[16,128]{1,0:T(8,128)} %get-tuple-element.8) | copy-start | bytes 24580

commit v2 on v1

--- a/solution.py
+++ b/solution.py
@@ -10,9 +10,9 @@
 NDYN = 4
 NSUB = 8
 GROUPS = 2
-UNROLL = 2
-MICRO = 4
-SOLVE = 4
+UNROLL = 4
+MICRO = 8
+SOLVE = 8
 MESH = pl.DeviceIdType.MESH
 LOG2E = 1.4426950408889634
 GAIN = 0.25 * LOG2E

time: 40.9 us -> 37.1 us (0.907)
  Pallas kernels: 37 us -> 33.2 us
    pallas_call x1, Pallas kernels: 37 us -> 33.2 us  [on_device(): pl.pallas_call(functools.partial(kernel, nlat, nlon, levels, rows), out_s...]
where the time goes in v2:
time: 37.1 us; the launch traced here: 36.9 us
  Pallas kernels  33.2 us (89%)
  local copies, waits for them, and re-layouts  3.02 us (8%)
  between operations  0.65 us (2%)
    pallas_call x1, Pallas kernels, on_device(): pl.pallas_call(functools.partial(kernel, nlat, nlon, levels, rows), out_s...  33.2 us
    unnamed x7, local copies, waits for them, and re-layouts  3.02 us

profile of v2, /device:TPU:0, one launch (start us, length us, event | category | flops | bytes accessed | tf_op | source)
XLA Modules:
  0.0 36.9 jit_solution(8141249551668553592)
XLA Ops:
  0.6 33.2 %shard_map.112 = (f32[512,128]{1,0:T(8,128)}, f32[512,128]{1,0:T(8,128)}, f32[16,128]{1,0:T(8,128)}) custom-call(f32[512,128]{1,0:T(8,128)} %bitcast.10, f32[512,128]{1,0:T(8,128)} %bitcast.11, f32[512,128]{1,0:T(8,128)} %bitcast.12, f32[512,128]{1,0:T(8,128)} %bitcast.13, f32[512,128]{1,0:T(8,128)} %bitcast.14, f32[512,128]{1,0:T(8,128)} %bitcast.15, ...), custom_call_target="tpu_custom_call" | custom-call | tf_op jit(solution)/shard_map/pallas_call | solution.py:517
  33.9 0.0 copy-start
  33.9 1.7 %copy.15 = f32[32,16,128]{2,1,0:T(8,128)} copy(f32[32,16,128]{2,1,0:T(8,128)} %bitcast.18) | data formatting | bytes 524288
  35.6 0.0 copy-done
  35.6 0.0 copy-start.1
  35.6 0.7 %copy.16 = f32[32,16,128]{2,1,0:T(8,128)} copy(f32[32,16,128]{2,1,0:T(8,128)S(1)} %bitcast.17) | data formatting | bytes 524288
  36.3 0.0 copy-done.1
  36.3 0.6 %copy.17 = f32[1,2048]{1,0:T(1,128)} copy(f32[1,2048]{1,0:T(1,128)S(1)} %bitcast.19) | data formatting | bytes 16384
Async XLA Ops:
  33.9 1.7 %copy-start = (f32[512,128]{1,0:T(8,128)S(1)}, f32[512,128]{1,0:T(8,128)}, u32[]{:S(2)}) copy-start(f32[512,128]{1,0:T(8,128)} %get-tuple-element.7) | copy-start | bytes 786436
  35.6 0.7 %copy-start.1 = (f32[16,128]{1,0:T(8,128)S(1)}, f32[16,128]{1,0:T(8,128)}, u32[]{:S(2)}) copy-start(f32[16,128]{1,0:T(8,128)} %get-tuple-element.8) | copy-start | bytes 24580

commit v3 on v2

--- a/solution.py
+++ b/solution.py
@@ -10,7 +10,7 @@
 NDYN = 4
 NSUB = 8
 GROUPS = 2
-UNROLL = 4
+UNROLL = 8
 MICRO = 8
 SOLVE = 8
 MESH = pl.DeviceIdType.MESH

time: 37.1 us -> 36.9 us (level)
  no operation moved by 1% of the time
where the time goes in v3:
time: 36.9 us; the launch traced here: 36.7 us
  Pallas kernels  33 us (89%)
  local copies, waits for them, and re-layouts  3.02 us (8%)
  between operations  0.65 us (2%)
    pallas_call x1, Pallas kernels, on_device(): pl.pallas_call(functools.partial(kernel, nlat, nlon, levels, rows), out_s...  33 us
    unnamed x7, local copies, waits for them, and re-layouts  3.02 us

profile of v3, /device:TPU:0, one launch (start us, length us, event | category | flops | bytes accessed | tf_op | source)
XLA Modules:
  0.0 36.7 jit_solution(13138627040145868013)
XLA Ops:
  0.6 33.0 %shard_map.112 = (f32[512,128]{1,0:T(8,128)}, f32[512,128]{1,0:T(8,128)}, f32[16,128]{1,0:T(8,128)}) custom-call(f32[512,128]{1,0:T(8,128)} %bitcast.10, f32[512,128]{1,0:T(8,128)} %bitcast.11, f32[512,128]{1,0:T(8,128)} %bitcast.12, f32[512,128]{1,0:T(8,128)} %bitcast.13, f32[512,128]{1,0:T(8,128)} %bitcast.14, f32[512,128]{1,0:T(8,128)} %bitcast.15, ...), custom_call_target="tpu_custom_call" | custom-call | tf_op jit(solution)/shard_map/pallas_call | solution.py:517
  33.7 0.0 copy-start
  33.7 1.7 %copy.15 = f32[32,16,128]{2,1,0:T(8,128)} copy(f32[32,16,128]{2,1,0:T(8,128)} %bitcast.18) | data formatting | bytes 524288
  35.4 0.0 copy-done
  35.4 0.0 copy-start.1
  35.4 0.7 %copy.16 = f32[32,16,128]{2,1,0:T(8,128)} copy(f32[32,16,128]{2,1,0:T(8,128)S(1)} %bitcast.17) | data formatting | bytes 524288
  36.1 0.0 copy-done.1
  36.1 0.6 %copy.17 = f32[1,2048]{1,0:T(1,128)} copy(f32[1,2048]{1,0:T(1,128)S(1)} %bitcast.19) | data formatting | bytes 16384
Async XLA Ops:
  33.7 1.7 %copy-start = (f32[512,128]{1,0:T(8,128)S(1)}, f32[512,128]{1,0:T(8,128)}, u32[]{:S(2)}) copy-start(f32[512,128]{1,0:T(8,128)} %get-tuple-element.7) | copy-start | bytes 786436
  35.4 0.7 %copy-start.1 = (f32[16,128]{1,0:T(8,128)S(1)}, f32[16,128]{1,0:T(8,128)}, u32[]{:S(2)}) copy-start(f32[16,128]{1,0:T(8,128)} %get-tuple-element.8) | copy-start | bytes 24580
